TPU v7x, 32 devices: a whole 2x2x4 slice. The times are simulated.
32 devices in a mesh: sy: 4 (over z), sx: 4 (over y, core), tp: 2 (over x).
Axes of the slice: x: 2, y: 2, z: 4, core: 2. Of those that a mesh axis runs over, the one named last changes fastest.
Arguments:
- features: bfloat16 [96, 64, 1408], P('sy', 'sx', 'tp'), may hold values from -6 to 6
- depth_kernel: float32 [7, 7, 1408], P(None, None, 'tp'), may hold values from -0.875 to 0.875
- depth_bias: float32 [1408], P('tp'), may hold values from -1 to 1
- norm_gain: float32 [1408], replicated, may hold values from 0.1 to 1.9
- norm_bias: float32 [1408], replicated, may hold values from -3 to 3
- up_weight: bfloat16 [1408, 5632], P(None, 'tp'), may hold values from -0.15625 to 0.15625
- up_bias: float32 [5632], P('tp'), may hold values from -3 to 3
- response_gain: float32 [5632], P('tp'), may hold values from -4 to 4
- response_shift: float32 [5632], P('tp'), may hold values from -3 to 3
- down_weight: bfloat16 [5632, 1408], P('tp', ('sy', 'sx')), may hold values from -0.078125 to 0.078125
- down_bias: float32 [1408], P('tp'), may hold values from -3 to 3
- tissue: int32 [12, 8], P('sy', 'sx'), may hold values from 0 to 1, as said below
- cotangent: bfloat16 [96, 64, 1408], P('sy', 'sx', 'tp'), may hold values from -6 to 6
Outputs:
- block_out: bfloat16 [96, 64, 1408], P('sy', 'sx', 'tp')
- feature_grad: bfloat16 [96, 64, 1408], P('sy', 'sx', 'tp')
Inputs may be any that keep to these rules, and one draw needn't show every extreme that they name: Each device's block of 3 x 2 tiles holds 1 to 4 tissue tiles; some device's block holds exactly 4.
All inputs are finite; a program needn't handle non-finite values.
Results may differ from a plain program's by a relative error of at most 0.0049.
The roundings to bfloat16 on the way count: a program that leaves them out, or rounds other values in their place, can miss the bound.
Values may be sent and summed in bfloat16 or wider, within the bound.
A program may use at most 128 MiB of HBM per device.

v0:
```python
import jax
import jax.numpy as jnp
from jax import lax
from jax.sharding import PartitionSpec as P

KERNEL = 7
TILE = 8
root_half = 0.7071067811865476
root_two_pi_inv = 0.3989422804014327


def extended(block, sides, width):
    for axis, dim in sides:
        count = lax.axis_size(axis)
        forward = [(i, i + 1) for i in range(count - 1)]
        backward = [(target, source) for source, target in forward]
        low = lax.ppermute(
            lax.slice_in_dim(block, block.shape[dim] - width, None, axis=dim), axis, forward
        )
        high = lax.ppermute(lax.slice_in_dim(block, 0, width, axis=dim), axis, backward)
        block = jnp.concatenate([low, block, high], axis=dim)
    return block


def gelu_value(values):
    return 0.5 * values * (1.0 + jax.scipy.special.erf(values * root_half))


def gelu_slope(values):
    return (
        0.5 * (1.0 + jax.scipy.special.erf(values * root_half))
        + values * jnp.exp(-0.5 * values * values) * root_two_pi_inv
    )


def depthwise(padded, kernel, rows_out, cols_out, flipped):
    summed = jnp.zeros((rows_out, cols_out, kernel.shape[2]), jnp.float32)
    last_tap = KERNEL - 1
    for row_tap in range(KERNEL):
        for col_tap in range(KERNEL):
            row_start = last_tap - row_tap if flipped else row_tap
            col_start = last_tap - col_tap if flipped else col_tap
            window = padded[row_start : row_start + rows_out, col_start : col_start + cols_out]
            summed = summed + window.astype(jnp.float32) * kernel[row_tap, col_tap]
    return summed


def extend(image):
    return extended(image, (("sy", 0), ("sx", 1)), KERNEL // 2)


def all_channels(rows_array):
    return lax.all_gather(rows_array, "tp", axis=1, tiled=True)


def global_vector(local_part):
    hidden_local = local_part.shape[0]
    placed = lax.dynamic_update_slice(
        jnp.zeros((hidden_local * lax.axis_size("tp"),), jnp.float32),
        local_part,
        (lax.axis_index("tp") * hidden_local,),
    )
    return lax.psum(placed, ("sy", "sx", "tp"))


def shards(
    features,
    depth_kernel,
    depth_bias,
    norm_gain,
    norm_bias,
    up_weight,
    up_bias,
    response_gain,
    response_shift,
    down_weight,
    down_bias,
    tissue,
    cotangent,
):
    image_rows, image_cols, local_channels = features.shape
    hidden_local = up_weight.shape[1]
    channel_start = lax.axis_index("tp") * local_channels
    contract_last = (((1,), (1,)), ((), ()))
    pixel_mask = jnp.repeat(jnp.repeat(tissue, TILE, axis=0), TILE, axis=1).astype(jnp.float32)
    mask_rows = pixel_mask.reshape(-1)

    def select(image):
        return image.reshape(image_rows * image_cols, image.shape[2])

    def restore(rows_array):
        return rows_array.reshape(image_rows, image_cols, rows_array.shape[1])

    convolved = (
        depthwise(extend(features), depth_kernel, image_rows, image_cols, False) + depth_bias
    ).astype(jnp.bfloat16)
    gathered = all_channels(select(convolved)).astype(jnp.float32)
    centre = jnp.mean(gathered, axis=1, keepdims=True)
    spread = jnp.mean(jnp.square(gathered - centre), axis=1, keepdims=True)
    inv_scale = lax.rsqrt(spread + 1e-06)
    standard = (gathered - centre) * inv_scale
    normed = (standard * norm_gain + norm_bias).astype(jnp.bfloat16)
    preact = jnp.dot(normed, up_weight, preferred_element_type=jnp.float32) + up_bias
    hidden = gelu_value(preact).astype(jnp.bfloat16)
    hidden_wide = hidden.astype(jnp.float32)
    squares = global_vector(jnp.sum(mask_rows[:, None] * hidden_wide * hidden_wide, axis=0))
    all_norms = jnp.sqrt(squares)
    norm_level = jnp.mean(all_norms) + 1e-06
    unit_start = lax.axis_index("tp") * hidden_local
    column_norms = lax.dynamic_slice_in_dim(all_norms, unit_start, hidden_local)
    norm_ratio = column_norms / norm_level
    response = (response_gain * hidden_wide * norm_ratio + response_shift + hidden_wide).astype(
        jnp.bfloat16
    )
    down_whole = lax.all_gather(down_weight, ("sy", "sx"), axis=1, tiled=True)
    partial_out = jnp.dot(response, down_whole, preferred_element_type=jnp.float32)
    branch = lax.psum_scatter(partial_out, "tp", scatter_dimension=1, tiled=True)
    branch_image = restore(branch + down_bias)
    block_out = (features.astype(jnp.float32) + pixel_mask[:, :, None] * branch_image).astype(
        jnp.bfloat16
    )
    masked_cot = (select(cotangent).astype(jnp.float32) * mask_rows[:, None]).astype(jnp.bfloat16)
    cot_wide = all_channels(masked_cot)
    back_hidden = lax.dot_general(
        cot_wide, down_whole, contract_last, preferred_element_type=jnp.float32
    )
    ratio_grad = global_vector(response_gain * jnp.sum(back_hidden * hidden_wide, axis=0))
    ratio_local = lax.dynamic_slice_in_dim(ratio_grad, unit_start, hidden_local)
    norms_grad = ratio_local / norm_level - jnp.sum(ratio_grad * all_norms) / (
        all_norms.shape[0] * norm_level * norm_level
    )
    hidden_grad = (
        back_hidden * (response_gain * norm_ratio + 1.0)
        + norms_grad * mask_rows[:, None] * hidden_wide / column_norms
    )
    preact_grad = (hidden_grad * gelu_slope(preact)).astype(jnp.bfloat16)
    grad_terms = lax.dot_general(
        preact_grad, up_weight, contract_last, preferred_element_type=jnp.float32
    )
    normed_grad = lax.psum(grad_terms, "tp")
    scaled = normed_grad * norm_gain
    convolved_grad = inv_scale * (
        scaled
        - jnp.mean(scaled, axis=1, keepdims=True)
        - standard * jnp.mean(scaled * standard, axis=1, keepdims=True)
    )
    convolved_grad = convolved_grad.astype(jnp.bfloat16)
    local_grad = lax.dynamic_slice_in_dim(convolved_grad, channel_start, local_channels, 1)
    grad_image = restore(local_grad)
    feature_grad = (
        cotangent.astype(jnp.float32)
        + depthwise(extend(grad_image), depth_kernel, image_rows, image_cols, True)
    ).astype(jnp.bfloat16)
    return (block_out, feature_grad)


def solution(mesh):
    placed = (
        P("sy", "sx", "tp"),
        P(None, None, "tp"),
        P("tp"),
        P(),
        P(),
        P(None, "tp"),
        P("tp"),
        P("tp"),
        P("tp"),
        P("tp", ("sy", "sx")),
        P("tp"),
        P("sy", "sx"),
        P("sy", "sx", "tp"),
    )
    return jax.shard_map(
        shards,
        mesh=mesh,
        in_specs=placed,
        out_specs=(P("sy", "sx", "tp"), P("sy", "sx", "tp")),
        check_vma=False,
    )
```

profile of v0, /device:TPU:0, one launch (start us, length us, event | category | flops | bytes accessed | tf_op | source)
XLA Modules:
  0.0 338.2 jit_solution(16324802515780690744)
XLA Ops:
  8.1 4.9 %collective-permute-start = (bf16[3,16,704]{2,1,0:T(8,128)(2,1)S(1)}, bf16[3,16,704]{2,1,0:T(8,128)(2,1)S(1)}, u32[]{:S(2)}, u32[]{:S(2)}) collective-permute-start(bf16[3,16,704]{2,1,0:T(8,128)(2,1)S(1)} %get-tuple-element.77), channel_id=1, source_target_pairs={{0,8},{8,16},{16,24},{1,9},{9,17},{17,25},{2,10},{10,18},{18,26},{... | collective-permute-start | bytes 202760 | tf_op jit(solution)/shard_map/ppermute | solution.py:17
  14.4 1.4 slice_reduce_fusion.48
  19.5 1.3 collective-permute-start.2
  20.8 1.3 collective-permute-start.3
  22.1 1.4 slice_reduce_fusion.47
  23.5 2.4 collective-permute-done.3
  25.9 14.1 %add_convert_fusion.2 = bf16[24,16,704]{2,1,0:T(8,128)(2,1)S(1)} fusion(bf16[24,16,704]{2,1,0:T(8,128)(2,1)S(1)} %copy-done, bf16[30,16,704]{2,1,0:T(8,128)(2,1)S(1)} %get-tuple-element.81, bf16[30,3,704]{2,1,0:T(4,128)(2,1)S(1)} %collective-permute-done.3, bf16[30,3,704]{2,1,0:T(4,128)(2,1)S(1)} %collective-permute-done.2, ...), kind=kLoop, calls=%fused_computation.149 | loop fusion | flops 74072064 | bytes 5395456 | tf_op jit(solution)/shard_map/convert_element_type | solution.py:96
  43.5 23.3 %all-gather.4.cloned.1.call-done = bf16[384,1408]{0,1:T(8,128)(2,1)} async-done(((bf16[384,704]{0,1:T(8,128)(2,1)}), bf16[384,1408]{0,1:T(8,128)(2,1)}) %all-gather.4.cloned.1.call-update) | async-done | bytes 1081360 | tf_op jit(solution)/shard_map/all_gather | solution.py:53
  66.7 1.7 copy.22
  69.2 8.6 %convolution_add_fusion = f32[384,2816]{1,0:T(8,128)} fusion(bf16[1408,2816]{1,0:T(8,128)(2,1)} %param.18, f32[2816]{0:T(1024)S(1)} %copy-done.7, f32[1408]{0:T(1024)S(1)} %copy-done.9, f32[1408]{0:T(1024)S(1)} %copy-done.3, bf16[384,1408]{1,0:T(8,128)(2,1)S(1)} %copy.22, f32[384]{0:T(512)S(1)} %add_rsqrt_fusion, f32[384]{0:T(512)S(1)} %broadcast_multiply_fusion.3), kind=kOutput, calls=%fused_computation.62 | convolution fusion | flops 3049390080 | bytes 13362176 | tf_op jit(solution)/shard_map/dot_general | solution.py:103
  77.8 12.8 %all-gather.8.cloned.1.call-done = bf16[384,1408]{0,1:T(8,128)(2,1)} async-done(((bf16[384,704]{0,1:T(8,128)(2,1)}), bf16[384,1408]{0,1:T(8,128)(2,1)}) %all-gather.8.cloned.1.call-update) | async-done | bytes 1081360 | tf_op jit(solution)/shard_map/all_gather | solution.py:53
  90.6 74.2 %all-gather.6.cloned.1.call-done = bf16[2816,1408]{0,1:T(8,128)(2,1)} async-done(((bf16[2816,88]{0,1:T(8,128)(2,1)}), bf16[2816,1408]{0,1:T(8,128)(2,1)}) %all-gather.6.cloned.1.call-update) | async-done | bytes 7929872 | tf_op jit(solution)/shard_map/all_gather | solution.py:115
  164.8 9.9 %fusion.10 = (f32[2816]{0:T(1024)S(1)}, f32[2816]{0:T(1024)S(1)}, bf16[384,2816]{1,0:T(8,128)(2,1)}, f32[384,2816]{1,0:T(8,128)}) fusion(f32[384]{0:T(512)S(1)} %convert_element_type.419, f32[384,2816]{1,0:T(8,128)} %convolution_add_fusion, bf16[384,1408]{0,1:T(8,128)(2,1)} %all-gather.8.cloned.1.call-done, bf16[2816,1408]{0,1:T(8,128)(2,1)} %all-gather.6.cloned.1.call-done), kind=kOutput, calls=%fused_computation.57 | convolution fusion | flops 3056953856 | bytes 19848704 | tf_op jit(solution)/shard_map/dot_general | solution.py:124
  175.2 39.6 %all-reduce = (f32[5632]{0:T(1024)S(1)}, f32[5632]{0:T(1024)S(1)}) all-reduce(f32[5632]{0:T(1024)S(1)} %dynamic_update_slice.6, f32[5632]{0:T(1024)S(1)} %multiply_dynamic-update-slice_fusion), channel_id=1, replica_groups=mesh['sy'=4,'sx'=4,'tp'=2] {'sy','sx','tp'}, use_global_device_ids=true, to_apply=%region_3.0 | all-reduce | flops 11264 | bytes 90112 | tf_op jit(solution)/shard_map/psum | solution.py:63
  216.7 12.4 %fusion.21 = f32[384,1408]{1,0:T(8,128)} fusion(bf16[1408,2816]{1,0:T(8,128)(2,1)} %param.18, f32[384,2816]{1,0:T(8,128)} %convolution_add_fusion, bf16[384,2816]{1,0:T(8,128)(2,1)} %get-tuple-element.63, f32[384,2816]{1,0:T(8,128)} %get-tuple-element.83, f32[2816]{0:T(1024)S(1)} %get-tuple-element.62, f32[2816]{0:T(1024)S(1)} %get-tuple-element.84, ...), kind=kOutput, calls=%fused_computation.74 | convolution fusion | flops 3062366208 | bytes 20941312 | tf_op jit(solution)/shard_map/dot_general | solution.py:137
  229.8 9.6 %fusion.16 = f32[384,1408]{0,1:T(8,128)} fusion(bf16[2816,1408]{0,1:T(8,128)(2,1)} %all-gather.6.cloned.1.call-done, bf16[384,2816]{1,0:T(8,128)(2,1)} %get-tuple-element.63, f32[2816]{0:T(1024)S(1)} %copy-done.8, f32[2816]{0:T(1024)S(1)} %get-tuple-element.61, f32[2816]{0:T(1024)S(1)} %copy-done.2), kind=kOutput, calls=%fused_computation.68 | convolution fusion | flops 3051552768 | bytes 12289024 | tf_op jit(solution)/shard_map/dot_general | solution.py:116
  239.4 54.7 %all-reduce.3.cloned.1.call-done = f32[384,1408]{1,0:T(8,128)} async-done(((f32[384,1408]{1,0:T(8,128)}), f32[384,1408]{1,0:T(8,128)}) %all-reduce.3.cloned.1.call-update) | async-done | bytes 2162704 | tf_op jit(solution)/shard_map/psum | solution.py:140
  294.1 2.3 fusion.102
  297.4 3.4 %collective-permute-start.4 = (bf16[3,16,704]{2,1,0:T(8,128)(2,1)S(1)}, bf16[3,16,704]{2,1,0:T(8,128)(2,1)S(1)}, u32[]{:S(2)}, u32[]{:S(2)}) collective-permute-start(bf16[3,16,704]{2,1,0:T(8,128)(2,1)S(1)} %bitcast.23), channel_id=1, source_target_pairs={{0,8},{8,16},{16,24},{1,9},{9,17},{17,25},{2,10},{10,18},{18,26},{... | collective-permute-start | bytes 202760 | tf_op jit(solution)/shard_map/ppermute | solution.py:17
  302.7 4.3 %collective-permute-done.5 = bf16[3,16,704]{2,1,0:T(8,128)(2,1)S(1)} collective-permute-done((bf16[3,16,704]{2,1,0:T(8,128)(2,1)S(1)}, bf16[3,16,704]{2,1,0:T(8,128)(2,1)S(1)}, u32[]{:S(2)}, u32[]{:S(2)}) %collective-permute-start.5) | collective-permute-done | bytes 67616 | tf_op jit(solution)/shard_map/ppermute | solution.py:20
  308.5 3.3 collective-permute-start.7
  313.1 10.3 %add_convert_fusion.1 = bf16[24,16,704]{2,1,0:T(8,128)(2,1)} fusion(bf16[24,16,704]{2,1,0:T(8,128)(2,1)S(1)} %bitcast.18, bf16[3,16,704]{2,1,0:T(8,128)(2,1)S(1)} %collective-permute-done.4, bf16[3,16,704]{2,1,0:T(8,128)(2,1)S(1)} %collective-permute-done.5, bf16[30,19,704]{2,1,0:T(8,128)(2,1)S(1)} %get-tuple-element.66, ...), kind=kLoop, calls=%fused_computation.148 | loop fusion | flops 41902080 | bytes 24603392 | tf_op jit(solution)/shard_map/convert_element_type | solution.py:153
  323.5 5.4 %reduce-scatter.2.cloned.1.call-done = f32[384,704]{0,1:T(8,128)} async-done(((f32[384,1408]{0,1:T(8,128)}), f32[384,704]{0,1:T(8,128)}) %reduce-scatter.2.cloned.1.call-update) | async-done | bytes 1081360 | tf_op jit(solution)/shard_map/reduce_scatter | solution.py:117
  328.9 1.4 broadcast_add_fusion
  (74 shorter events, 19.1 us)
Async XLA Ops:
  7.2 59.6 %all-gather.4.cloned.1.call-start = ((), (), s32[]{:S(2)}) async-start(), calls=%async_computation.1 | async-start | bytes 1622016 | tf_op jit(solution)/shard_map/all_gather | solution.py:53
  8.1 8.8 %collective-permute-start = (bf16[3,16,704]{2,1,0:T(8,128)(2,1)S(1)}, bf16[3,16,704]{2,1,0:T(8,128)(2,1)S(1)}, u32[]{:S(2)}, u32[]{:S(2)}) collective-permute-start(bf16[3,16,704]{2,1,0:T(8,128)(2,1)S(1)} %get-tuple-element.77), channel_id=1, source_target_pairs={{0,8},{8,16},{16,24},{1,9},{9,17},{17,25},{2,10},{10,18},{18,26},{... | collective-permute-start | bytes 202760 | tf_op jit(solution)/shard_map/ppermute | solution.py:17
  13.1 6.2 %collective-permute-start.1 = (bf16[3,16,704]{2,1,0:T(8,128)(2,1)S(1)}, bf16[3,16,704]{2,1,0:T(8,128)(2,1)S(1)}, u32[]{:S(2)}, u32[]{:S(2)}) collective-permute-start(bf16[3,16,704]{2,1,0:T(8,128)(2,1)S(1)} %get-tuple-element.76), channel_id=1, source_target_pairs={{8,0},{16,8},{24,16},{9,1},{17,9},{25,17},{10,2},{18,10},{26,18},{... | collective-permute-start | bytes 202760 | tf_op jit(solution)/shard_map/ppermute | solution.py:20
  18.1 7.7 %copy-start = (bf16[24,16,704]{2,1,0:T(8,128)(2,1)S(1)}, bf16[24,16,704]{2,1,0:T(8,128)(2,1)}, u32[]{:S(2)}) copy-start(bf16[24,16,704]{2,1,0:T(8,128)(2,1)} %param.13) | copy-start | bytes 1622020
  18.1 7.7 %copy-start.5 = (f32[704]{0:T(1024)S(1)}, f32[704]{0:T(1024)}, u32[]{:S(2)}) copy-start(f32[704]{0:T(1024)} %param.15) | copy-start | bytes 8452
  19.5 4.0 %collective-permute-start.2 = (bf16[30,3,704]{2,1,0:T(4,128)(2,1)S(1)}, bf16[30,3,704]{2,1,0:T(4,128)(2,1)S(1)}, u32[]{:S(2)}, u32[]{:S(2)}) collective-permute-start(bf16[30,3,704]{2,1,0:T(4,128)(2,1)S(1)} %get-tuple-element.69), channel_id=1, source_target_pairs={{0,2},{2,4},{4,6},{1,3},{3,5},{5,7},{8,10},{10,12},{12,14},{9,11},... | collective-permute-start | bytes 380168 | tf_op jit(solution)/shard_map/ppermute | solution.py:17
  20.8 5.1 %collective-permute-start.3 = (bf16[30,3,704]{2,1,0:T(4,128)(2,1)S(1)}, bf16[30,3,704]{2,1,0:T(4,128)(2,1)S(1)}, u32[]{:S(2)}, u32[]{:S(2)}) collective-permute-start(bf16[30,3,704]{2,1,0:T(4,128)(2,1)S(1)} %get-tuple-element.70), channel_id=1, source_target_pairs={{2,0},{4,2},{6,4},{3,1},{5,3},{7,5},{10,8},{12,10},{14,12},{11,9},... | collective-permute-start | bytes 380168 | tf_op jit(solution)/shard_map/ppermute | solution.py:20
  40.0 1.1 copy-start.6
  40.0 1.6 copy-start.1
  41.0 49.5 %all-gather.8.cloned.1.call-start = ((), (), s32[]{:S(2)}) async-start(), calls=%async_computation.4 | async-start | bytes 1622016 | tf_op jit(solution)/shard_map/all_gather | solution.py:53
  42.7 122.1 %all-gather.6.cloned.1.call-start = ((), (), s32[]{:S(2)}) async-start(), calls=%async_computation.2 | async-start | bytes 8425472 | tf_op jit(solution)/shard_map/all_gather | solution.py:115
  43.4 250.7 %all-reduce.3.cloned.1.call-start = ((), (), s32[]{:S(2)}) async-start(), calls=%async_computation.5 | async-start | bytes 4325376 | tf_op jit(solution)/shard_map/psum | solution.py:140
  68.5 0.7 copy-start.3
  68.5 0.7 copy-start.7
  68.5 0.7 copy-start.9
  77.8 97.2 %copy-start.2 = (f32[2816]{0:T(1024)S(1)}, f32[2816]{0:T(1024)}, u32[]{:S(2)}) copy-start(f32[2816]{0:T(1024)} %param.20) | copy-start | bytes 33796
  229.1 0.7 copy-start.8
  229.1 99.8 %reduce-scatter.2.cloned.1.call-start = ((), (), s32[]{:S(2)}) async-start(), calls=%async_computation.3 | async-start | bytes 3244032 | tf_op jit(solution)/shard_map/reduce_scatter | solution.py:117
  297.4 5.4 %collective-permute-start.4 = (bf16[3,16,704]{2,1,0:T(8,128)(2,1)S(1)}, bf16[3,16,704]{2,1,0:T(8,128)(2,1)S(1)}, u32[]{:S(2)}, u32[]{:S(2)}) collective-permute-start(bf16[3,16,704]{2,1,0:T(8,128)(2,1)S(1)} %bitcast.23), channel_id=1, source_target_pairs={{0,8},{8,16},{16,24},{1,9},{9,17},{17,25},{2,10},{10,18},{18,26},{... | collective-permute-start | bytes 202760 | tf_op jit(solution)/shard_map/ppermute | solution.py:17
  300.8 6.2 %collective-permute-start.5 = (bf16[3,16,704]{2,1,0:T(8,128)(2,1)S(1)}, bf16[3,16,704]{2,1,0:T(8,128)(2,1)S(1)}, u32[]{:S(2)}, u32[]{:S(2)}) collective-permute-start(bf16[3,16,704]{2,1,0:T(8,128)(2,1)S(1)} %bitcast.22), channel_id=1, source_target_pairs={{8,0},{16,8},{24,16},{9,1},{17,9},{25,17},{10,2},{18,10},{26,18},{... | collective-permute-start | bytes 202760 | tf_op jit(solution)/shard_map/ppermute | solution.py:20
  307.2 4.7 %collective-permute-start.6 = (bf16[30,3,704]{2,1,0:T(4,128)(2,1)S(1)}, bf16[30,3,704]{2,1,0:T(4,128)(2,1)S(1)}, u32[]{:S(2)}, u32[]{:S(2)}) collective-permute-start(bf16[30,3,704]{2,1,0:T(4,128)(2,1)S(1)} %get-tuple-element.67), channel_id=1, source_target_pairs={{2,0},{4,2},{6,4},{3,1},{5,3},{7,5},{10,8},{12,10},{14,12},{11,9},... | collective-permute-start | bytes 380168 | tf_op jit(solution)/shard_map/ppermute | solution.py:20
  308.5 4.1 %collective-permute-start.7 = (bf16[30,3,704]{2,1,0:T(4,128)(2,1)S(1)}, bf16[30,3,704]{2,1,0:T(4,128)(2,1)S(1)}, u32[]{:S(2)}, u32[]{:S(2)}) collective-permute-start(bf16[30,3,704]{2,1,0:T(4,128)(2,1)S(1)} %get-tuple-element.68), channel_id=1, source_target_pairs={{0,2},{2,4},{4,6},{1,3},{3,5},{5,7},{8,10},{10,12},{12,14},{9,11},... | collective-permute-start | bytes 380168 | tf_op jit(solution)/shard_map/ppermute | solution.py:17
  313.1 15.8 %copy-start.4 = (f32[704]{0:T(1024)S(1)}, f32[704]{0:T(1024)}, u32[]{:S(2)}) copy-start(f32[704]{0:T(1024)} %param.23) | copy-start | bytes 8452
Sparse Core Ops, SparseCore 0:
  41.2 25.5 all-gather.3
  68.9 21.6 all-gather.7
  92.8 71.9 all-gather.5
  229.2 64.8 all-reduce.2
  296.3 32.5 reduce-scatter.1
where the time goes:
time: 339 us; the launch traced here: 338 us
  waiting for transfers between devices  180 us (53%)
  matrix products  40.4 us (12%)
  blocking collectives  39.6 us (12%)
  other arithmetic  33.2 us (10%)
  starting transfers between devices  18.3 us (5%)
  between operations  15.4 us (5%)
  local copies, waits for them, and re-layouts  11 us (3%)
    all_gather x1, waiting for transfers between devices, shards(): down_whole = lax.all_gather(down_weight, ('sy', 'sx'), axis=1, tiled=True)  74.2 us
    psum x1, waiting for transfers between devices, shards(): normed_grad = lax.psum(grad_terms, 'tp')  54.7 us
    psum x1, blocking collectives, global_vector(): return lax.psum(placed, ('sy', 'sx', 'tp'))  39.6 us
    all_gather x2, waiting for transfers between devices, all_channels(): return lax.all_gather(rows_array, 'tp', axis=1, tiled=True)  36 us
    convert_element_type x1, other arithmetic, shards(): convolved = (depthwise(extend(features), depth_kernel, image_rows, image_...  14.1 us
    ppermute x4, starting transfers between devices, extended(): lax.ppermute(lax.slice_in_dim(block, block.shape[dim] - width, None, axis...  12.9 us
    dot_general x1, matrix products, shards(): lax.dot_general(preact_grad, up_weight, contract_last, preferred_element_...  12.4 us
    convert_element_type x1, other arithmetic, shards(): feature_grad = (cotangent.astype(jnp.float32) + depthwise(extend(grad_ima...  10.3 us
  transfers between devices with their start and end apart: 13, of which 10 were waited for; matrix products, arithmetic and copies ran while one was open for 12% of the time, Pallas kernels for 0%

commit v1 on v0

--- a/solution.py
+++ b/solution.py
@@ -137,7 +137,7 @@
     grad_terms = lax.dot_general(
         preact_grad, up_weight, contract_last, preferred_element_type=jnp.float32
     )
-    normed_grad = lax.psum(grad_terms, "tp")
+    normed_grad = jnp.sum(lax.all_gather(grad_terms, "tp"), axis=0)
     scaled = normed_grad * norm_gain
     convolved_grad = inv_scale * (
         scaled

time: 339 us -> 355 us (1.047)
  waiting for transfers between devices: 180 us -> 187 us
  other arithmetic: 33.2 us -> 38.1 us
    psum x1 -> x0, waiting for transfers between devices: 54.7 us -> none  [shards(): normed_grad = lax.psum(grad_terms, 'tp')]
    all_gather x0 -> x1, waiting for transfers between devices: none -> 48.4 us  [shards(): normed_grad = jnp.sum(lax.all_gather(grad_terms, 'tp'), axis=0)]
    reduce_scatter x1, waiting for transfers between devices: 5.44 us -> 24.9 us  [shards(): lax.psum_scatter(partial_out, 'tp', scatter_dimension=1, tiled=True)]
    ppermute x4, waiting for transfers between devices: 7.82 us -> 2.59 us  [extended(): lax.ppermute(lax.slice_in_dim(block, 0, width, axis=dim), axis, backward)]
  transfers between devices with their start and end apart: 13 -> 13, of which waited for: 10 -> 7; matrix products, arithmetic and copies ran while one was open for 12% -> 10% of each run, Pallas kernels for 0% -> 0%
where the time goes in v1:
time: 355 us; the launch traced here: 353 us
  waiting for transfers between devices  187 us (53%)
  matrix products  40.5 us (11%)
  blocking collectives  39.6 us (11%)
  other arithmetic  38.1 us (11%)
  starting transfers between devices  18.2 us (5%)
  between operations  16.7 us (5%)
  local copies, waits for them, and re-layouts  12.6 us (4%)
    all_gather x1, waiting for transfers between devices, shards(): down_whole = lax.all_gather(down_weight, ('sy', 'sx'), axis=1, tiled=True)  74.2 us
    all_gather x1, waiting for transfers between devices, shards(): normed_grad = jnp.sum(lax.all_gather(grad_terms, 'tp'), axis=0)  48.4 us
    psum x1, blocking collectives, global_vector(): return lax.psum(placed, ('sy', 'sx', 'tp'))  39.6 us
    all_gather x2, waiting for transfers between devices, all_channels(): return lax.all_gather(rows_array, 'tp', axis=1, tiled=True)  36.3 us
    reduce_scatter x1, waiting for transfers between devices, shards(): lax.psum_scatter(partial_out, 'tp', scatter_dimension=1, tiled=True)  24.9 us
    convert_element_type x1, other arithmetic, shards(): convolved = (depthwise(extend(features), depth_kernel, image_rows, image_...  15.1 us
    ppermute x4, starting transfers between devices, extended(): lax.ppermute(lax.slice_in_dim(block, block.shape[dim] - width, None, axis...  12.9 us
    dot_general x1, matrix products, shards(): lax.dot_general(preact_grad, up_weight, contract_last, preferred_element_...  12.4 us
  transfers between devices with their start and end apart: 13, of which 7 were waited for; matrix products, arithmetic and copies ran while one was open for 10% of the time, Pallas kernels for 0%

profile of v1, /device:TPU:0, one launch (start us, length us, event | category | flops | bytes accessed | tf_op | source)
XLA Modules:
  0.0 352.8 jit_solution(1323382839951348621)
XLA Ops:
  8.1 4.9 %collective-permute-start = (bf16[3,16,704]{2,1,0:T(8,128)(2,1)S(1)}, bf16[3,16,704]{2,1,0:T(8,128)(2,1)S(1)}, u32[]{:S(2)}, u32[]{:S(2)}) collective-permute-start(bf16[3,16,704]{2,1,0:T(8,128)(2,1)S(1)} %get-tuple-element.77), channel_id=1, source_target_pairs={{0,8},{8,16},{16,24},{1,9},{9,17},{17,25},{2,10},{10,18},{18,26},{... | collective-permute-start | bytes 202760 | tf_op jit(solution)/shard_map/ppermute | solution.py:17
  14.4 1.4 slice_reduce_fusion.48
  19.5 1.3 collective-permute-start.2
  20.8 1.3 collective-permute-start.3
  22.1 2.0 slice_reduce_fusion.47
  24.2 1.6 collective-permute-done.3
  26.1 15.1 %add_convert_fusion.2 = bf16[24,16,704]{2,1,0:T(8,128)(2,1)S(1)} fusion(bf16[24,16,704]{2,1,0:T(8,128)(2,1)S(1)} %copy-done, bf16[30,16,704]{2,1,0:T(8,128)(2,1)S(1)} %get-tuple-element.81, bf16[30,3,704]{2,1,0:T(4,128)(2,1)S(1)} %collective-permute-done.3, bf16[30,3,704]{2,1,0:T(4,128)(2,1)S(1)} %collective-permute-done.2, ...), kind=kLoop, calls=%fused_computation.149 | loop fusion | flops 74072064 | bytes 5395456 | tf_op jit(solution)/shard_map/convert_element_type | solution.py:96
  44.9 23.5 %all-gather.6.cloned.1.call-done = bf16[384,1408]{0,1:T(8,128)(2,1)} async-done(((bf16[384,704]{0,1:T(8,128)(2,1)}), bf16[384,1408]{0,1:T(8,128)(2,1)}) %all-gather.6.cloned.1.call-update) | async-done | bytes 1081360 | tf_op jit(solution)/shard_map/all_gather | solution.py:53
  68.4 1.7 copy.30
  70.8 8.6 %convolution_add_fusion = f32[384,2816]{1,0:T(8,128)} fusion(bf16[1408,2816]{1,0:T(8,128)(2,1)} %param.18, f32[2816]{0:T(1024)S(1)} %copy-done.87, f32[1408]{0:T(1024)S(1)} %copy-done.89, f32[1408]{0:T(1024)S(1)} %copy-done.83, bf16[384,1408]{1,0:T(8,128)(2,1)S(1)} %copy.30, f32[384]{0:T(512)S(1)} %add_rsqrt_fusion, f32[384]{0:T(512)S(1)} %broadcast_multiply_fusion.3), kind=kOutput, calls=%fused_computation.62 | convolution fusion | flops 3049390080 | bytes 13362176 | tf_op jit(solution)/shard_map/dot_general | solution.py:103
  79.4 12.8 %all-gather.10.cloned.1.call-done = bf16[384,1408]{0,1:T(8,128)(2,1)} async-done(((bf16[384,704]{0,1:T(8,128)(2,1)}), bf16[384,1408]{0,1:T(8,128)(2,1)}) %all-gather.10.cloned.1.call-update) | async-done | bytes 1081360 | tf_op jit(solution)/shard_map/all_gather | solution.py:53
  92.2 74.2 %all-gather.8.cloned.1.call-done = bf16[2816,1408]{0,1:T(8,128)(2,1)} async-done(((bf16[2816,88]{0,1:T(8,128)(2,1)}), bf16[2816,1408]{0,1:T(8,128)(2,1)}) %all-gather.8.cloned.1.call-update) | async-done | bytes 7929872 | tf_op jit(solution)/shard_map/all_gather | solution.py:115
  166.4 9.9 %fusion.10 = (f32[2816]{0:T(1024)S(1)}, f32[2816]{0:T(1024)S(1)}, bf16[384,2816]{1,0:T(8,128)(2,1)}, f32[384,2816]{1,0:T(8,128)}) fusion(f32[384]{0:T(512)S(1)} %convert_element_type.419, f32[384,2816]{1,0:T(8,128)} %convolution_add_fusion, bf16[384,1408]{0,1:T(8,128)(2,1)} %all-gather.10.cloned.1.call-done, bf16[2816,1408]{0,1:T(8,128)(2,1)} %all-gather.8.cloned.1.call-done), kind=kOutput, calls=%fused_computation.57 | convolution fusion | flops 3056953856 | bytes 19848704 | tf_op jit(solution)/shard_map/dot_general | solution.py:124
  176.8 39.6 %all-reduce = (f32[5632]{0:T(1024)S(1)}, f32[5632]{0:T(1024)S(1)}) all-reduce(f32[5632]{0:T(1024)S(1)} %dynamic_update_slice.6, f32[5632]{0:T(1024)S(1)} %multiply_dynamic-update-slice_fusion), channel_id=1, replica_groups=mesh['sy'=4,'sx'=4,'tp'=2] {'sy','sx','tp'}, use_global_device_ids=true, to_apply=%region_3.0 | all-reduce | flops 11264 | bytes 90112 | tf_op jit(solution)/shard_map/psum | solution.py:63
  218.3 12.4 %fusion.21 = f32[384,1408]{1,0:T(8,128)} fusion(bf16[1408,2816]{1,0:T(8,128)(2,1)} %param.18, f32[384,2816]{1,0:T(8,128)} %convolution_add_fusion, bf16[384,2816]{1,0:T(8,128)(2,1)} %get-tuple-element.63, f32[384,2816]{1,0:T(8,128)} %get-tuple-element.83, f32[2816]{0:T(1024)S(1)} %get-tuple-element.62, f32[2816]{0:T(1024)S(1)} %get-tuple-element.84, ...), kind=kOutput, calls=%fused_computation.74 | convolution fusion | flops 3062366208 | bytes 20941312 | tf_op jit(solution)/shard_map/dot_general | solution.py:137
  231.4 9.6 %fusion.16 = f32[384,1408]{0,1:T(8,128)} fusion(bf16[2816,1408]{0,1:T(8,128)(2,1)} %all-gather.8.cloned.1.call-done, bf16[384,2816]{1,0:T(8,128)(2,1)} %get-tuple-element.63, f32[2816]{0:T(1024)S(1)} %copy-done.88, f32[2816]{0:T(1024)S(1)} %get-tuple-element.61, f32[2816]{0:T(1024)S(1)} %copy-done.4), kind=kOutput, calls=%fused_computation.68 | convolution fusion | flops 3051552768 | bytes 12289024 | tf_op jit(solution)/shard_map/dot_general | solution.py:116
  241.2 48.4 %all-gather.12.cloned.1.call-done = f32[768,1408]{1,0:T(8,128)} async-done(((f32[384,1408]{1,0:T(8,128)}), f32[768,1408]{1,0:T(8,128)}) %all-gather.12.cloned.1.call-update) | async-done | bytes 4325392 | tf_op jit(solution)/shard_map/all_gather | solution.py:140
  289.6 2.7 reduce_sum.87
  294.7 3.4 collective-permute-start.4
  299.4 24.9 %reduce-scatter.2.cloned.1.call-done = f32[384,704]{0,1:T(8,128)} async-done(((f32[384,1408]{0,1:T(8,128)}), f32[384,704]{0,1:T(8,128)}) %reduce-scatter.2.cloned.1.call-update) | async-done | bytes 1081360 | tf_op jit(solution)/shard_map/reduce_scatter | solution.py:117
  324.3 1.4 broadcast_add_fusion
  328.4 3.3 collective-permute-start.7
  333.1 1.5 pad_maximum_fusion
  335.0 11.3 %add_convert_fusion.1 = bf16[24,16,704]{2,1,0:T(8,128)(2,1)} fusion(bf16[24,16,704]{2,1,0:T(8,128)(2,1)S(1)} %bitcast.19, bf16[3,16,704]{2,1,0:T(8,128)(2,1)S(1)} %collective-permute-done.4, bf16[3,16,704]{2,1,0:T(8,128)(2,1)} %collective-permute-done.5, bf16[30,19,704]{2,1,0:T(8,128)(2,1)S(1)} %get-tuple-element.66, ...), kind=kLoop, calls=%fused_computation.148 | loop fusion | flops 41902080 | bytes 24603392 | tf_op jit(solution)/shard_map/convert_element_type | solution.py:153
  (235 shorter events, 19.4 us)
Async XLA Ops:
  7.2 61.2 %all-gather.6.cloned.1.call-start = ((), (), s32[]{:S(2)}) async-start(), calls=%async_computation.1 | async-start | bytes 1622016 | tf_op jit(solution)/shard_map/all_gather | solution.py:53
  8.1 9.0 %collective-permute-start = (bf16[3,16,704]{2,1,0:T(8,128)(2,1)S(1)}, bf16[3,16,704]{2,1,0:T(8,128)(2,1)S(1)}, u32[]{:S(2)}, u32[]{:S(2)}) collective-permute-start(bf16[3,16,704]{2,1,0:T(8,128)(2,1)S(1)} %get-tuple-element.77), channel_id=1, source_target_pairs={{0,8},{8,16},{16,24},{1,9},{9,17},{17,25},{2,10},{10,18},{18,26},{... | collective-permute-start | bytes 202760 | tf_op jit(solution)/shard_map/ppermute | solution.py:17
  13.1 6.2 %collective-permute-start.1 = (bf16[3,16,704]{2,1,0:T(8,128)(2,1)S(1)}, bf16[3,16,704]{2,1,0:T(8,128)(2,1)S(1)}, u32[]{:S(2)}, u32[]{:S(2)}) collective-permute-start(bf16[3,16,704]{2,1,0:T(8,128)(2,1)S(1)} %get-tuple-element.76), channel_id=1, source_target_pairs={{8,0},{16,8},{24,16},{9,1},{17,9},{25,17},{10,2},{18,10},{26,18},{... | collective-permute-start | bytes 202760 | tf_op jit(solution)/shard_map/ppermute | solution.py:20
  19.5 4.7 %collective-permute-start.2 = (bf16[30,3,704]{2,1,0:T(4,128)(2,1)S(1)}, bf16[30,3,704]{2,1,0:T(4,128)(2,1)S(1)}, u32[]{:S(2)}, u32[]{:S(2)}) collective-permute-start(bf16[30,3,704]{2,1,0:T(4,128)(2,1)S(1)} %get-tuple-element.69), channel_id=1, source_target_pairs={{0,2},{2,4},{4,6},{1,3},{3,5},{5,7},{8,10},{10,12},{12,14},{9,11},... | collective-permute-start | bytes 380168 | tf_op jit(solution)/shard_map/ppermute | solution.py:17
  20.8 5.1 %collective-permute-start.3 = (bf16[30,3,704]{2,1,0:T(4,128)(2,1)S(1)}, bf16[30,3,704]{2,1,0:T(4,128)(2,1)S(1)}, u32[]{:S(2)}, u32[]{:S(2)}) collective-permute-start(bf16[30,3,704]{2,1,0:T(4,128)(2,1)S(1)} %get-tuple-element.70), channel_id=1, source_target_pairs={{2,0},{4,2},{6,4},{3,1},{5,3},{7,5},{10,8},{12,10},{14,12},{11,9},... | collective-permute-start | bytes 380168 | tf_op jit(solution)/shard_map/ppermute | solution.py:20
  24.1 17.1 %copy-start.61 = (f32[704]{0:T(1024)}, f32[704]{0:T(1024)S(1)}, u32[]{:S(2)}) copy-start(f32[704]{0:T(1024)S(1)} %get-tuple-element.30) | copy-start | bytes 8452
  24.1 17.1 %copy-start.63 = (f32[704]{0:T(1024)}, f32[704]{0:T(1024)S(1)}, u32[]{:S(2)}) copy-start(f32[704]{0:T(1024)S(1)} %get-tuple-element.31) | copy-start | bytes 8452
  24.1 17.1 %copy-start.65 = (f32[704]{0:T(1024)}, f32[704]{0:T(1024)S(1)}, u32[]{:S(2)}) copy-start(f32[704]{0:T(1024)S(1)} %get-tuple-element.32) | copy-start | bytes 8452
  24.1 17.1 %copy-start.67 = (f32[704]{0:T(1024)}, f32[704]{0:T(1024)S(1)}, u32[]{:S(2)}) copy-start(f32[704]{0:T(1024)S(1)} %get-tuple-element.33) | copy-start | bytes 8452
  24.2 17.1 %copy-start.69 = (f32[704]{0:T(1024)}, f32[704]{0:T(1024)S(1)}, u32[]{:S(2)}) copy-start(f32[704]{0:T(1024)S(1)} %get-tuple-element.34) | copy-start | bytes 8452
  24.2 17.1 %copy-start.71 = (f32[704]{0:T(1024)}, f32[704]{0:T(1024)S(1)}, u32[]{:S(2)}) copy-start(f32[704]{0:T(1024)S(1)} %get-tuple-element.35) | copy-start | bytes 8452
  24.2 17.1 %copy-start.73 = (f32[704]{0:T(1024)}, f32[704]{0:T(1024)S(1)}, u32[]{:S(2)}) copy-start(f32[704]{0:T(1024)S(1)} %get-tuple-element.36) | copy-start | bytes 8452
  24.2 17.1 %copy-start.75 = (f32[704]{0:T(1024)}, f32[704]{0:T(1024)S(1)}, u32[]{:S(2)}) copy-start(f32[704]{0:T(1024)S(1)} %get-tuple-element.37) | copy-start | bytes 8452
  24.2 17.1 %copy-start.77 = (f32[704]{0:T(1024)}, f32[704]{0:T(1024)S(1)}, u32[]{:S(2)}) copy-start(f32[704]{0:T(1024)S(1)} %get-tuple-element.38) | copy-start | bytes 8452
  42.4 49.8 %all-gather.10.cloned.1.call-start = ((), (), s32[]{:S(2)}) async-start(), calls=%async_computation.4 | async-start | bytes 1622016 | tf_op jit(solution)/shard_map/all_gather | solution.py:53
  44.1 122.3 %all-gather.8.cloned.1.call-start = ((), (), s32[]{:S(2)}) async-start(), calls=%async_computation.2 | async-start | bytes 8425472 | tf_op jit(solution)/shard_map/all_gather | solution.py:115
  44.8 244.8 %all-gather.12.cloned.1.call-start = ((), (), s32[]{:S(2)}) async-start(), calls=%async_computation.5 | async-start | bytes 6488064 | tf_op jit(solution)/shard_map/all_gather | solution.py:140
  79.4 97.2 %copy-start.4 = (f32[2816]{0:T(1024)S(1)}, f32[2816]{0:T(1024)}, u32[]{:S(2)}) copy-start(f32[2816]{0:T(1024)} %param.20) | copy-start | bytes 33796
  230.7 93.6 %reduce-scatter.2.cloned.1.call-start = ((), (), s32[]{:S(2)}) async-start(), calls=%async_computation.3 | async-start | bytes 3244032 | tf_op jit(solution)/shard_map/reduce_scatter | solution.py:117
  293.0 31.3 %copy-start.84 = (f32[704]{0:T(1024)S(1)}, f32[704]{0:T(1024)}, u32[]{:S(2)}) copy-start(f32[704]{0:T(1024)} %param.23) | copy-start | bytes 8452
  294.7 31.4 %collective-permute-start.4 = (bf16[3,16,704]{2,1,0:T(8,128)(2,1)}, bf16[3,16,704]{2,1,0:T(8,128)(2,1)S(1)}, u32[]{:S(2)}, u32[]{:S(2)}) collective-permute-start(bf16[3,16,704]{2,1,0:T(8,128)(2,1)} %bitcast.5), channel_id=1, source_target_pairs={{0,8},{8,16},{16,24},{1,9},{9,17},{17,25},{2,10},{10,18},{18,26},{... | collective-permute-start | bytes 202760 | tf_op jit(solution)/shard_map/ppermute | solution.py:17
  298.1 28.0 %collective-permute-start.5 = (bf16[3,16,704]{2,1,0:T(8,128)(2,1)}, bf16[3,16,704]{2,1,0:T(8,128)(2,1)}, u32[]{:S(2)}, u32[]{:S(2)}) collective-permute-start(bf16[3,16,704]{2,1,0:T(8,128)(2,1)} %bitcast.7), channel_id=1, source_target_pairs={{8,0},{16,8},{24,16},{9,1},{17,9},{25,17},{10,2},{18,10},{26,18},{... | collective-permute-start | bytes 202760 | tf_op jit(solution)/shard_map/ppermute | solution.py:20
  327.1 6.0 %collective-permute-start.6 = (bf16[30,3,704]{2,1,0:T(4,128)(2,1)S(1)}, bf16[30,3,704]{2,1,0:T(4,128)(2,1)S(1)}, u32[]{:S(2)}, u32[]{:S(2)}) collective-permute-start(bf16[30,3,704]{2,1,0:T(4,128)(2,1)S(1)} %get-tuple-element.67), channel_id=1, source_target_pairs={{2,0},{4,2},{6,4},{3,1},{5,3},{7,5},{10,8},{12,10},{14,12},{11,9},... | collective-permute-start | bytes 380168 | tf_op jit(solution)/shard_map/ppermute | solution.py:20
  328.4 4.7 %collective-permute-start.7 = (bf16[30,3,704]{2,1,0:T(4,128)(2,1)S(1)}, bf16[30,3,704]{2,1,0:T(4,128)(2,1)S(1)}, u32[]{:S(2)}, u32[]{:S(2)}) collective-permute-start(bf16[30,3,704]{2,1,0:T(4,128)(2,1)S(1)} %get-tuple-element.68), channel_id=1, source_target_pairs={{0,2},{2,4},{4,6},{1,3},{3,5},{5,7},{8,10},{10,12},{12,14},{9,11},... | collective-permute-start | bytes 380168 | tf_op jit(solution)/shard_map/ppermute | solution.py:17
  (79 other events, 443.9 us)
Sparse Core Ops, SparseCore 0:
  42.5 25.7 all-gather.5
  70.5 21.6 all-gather.9
  94.4 71.9 all-gather.7
  230.9 58.6 all-gather.11
  291.7 32.5 reduce-scatter.1
